TPU v7x, 32 devices: a whole 2x2x4 slice. The times are simulated.
32 devices in a mesh: groups: 2 (over y), fsdp: 8 (over z, x), batch: 2 (over core).
Axes of the slice: x: 2, y: 2, z: 4, core: 2. Of those that a mesh axis runs over, the one named last changes fastest.
Arguments:
- activations: bfloat16 [2, 2048, 8192], P('batch', ('groups', 'fsdp')), parts along dimension 1, may hold values from -6 to 6
- cotangent: bfloat16 [2, 2048, 8192], P('batch', ('groups', 'fsdp')), parts along dimension 1, may hold values from -6 to 6
- adapter: bfloat16 [2, 8192, 128], P(None, 'fsdp'), may hold values from -0.0625 to 0.0625
- lengths: int32 [2, 4], P(None, 'groups'), parts along dimension 1, may hold values from 128 to 512, as said below
- layout: int32 [2, 16], P(None, 'groups'), parts along dimension 1, may hold values from 0 to 7, each once within a row
- feature_signs: int32 [2, 8192], replicated, may hold values from 0 to 1
- rank_signs: int32 [2, 128], replicated, may hold values from 0 to 1
- hadamard_rows: int32 [2, 8192], replicated, may hold values from 0 to 8191, each once within a row
- entry_pick: int32 [2, 4096], replicated, may hold values from 0 to 131071
- val_feats: float32 [512, 8192], P('groups', 'fsdp'), parts along dimension 0, may hold values from -600 to 600
Outputs:
- similarity: float32 [2, 4, 256], P('batch', 'groups'), parts along dimension 1
There are 2 independent parts, one for each index of `groups`. A program takes and returns all parts, laid end to end along the dimension named above; an argument that names none is the same for every part. Nothing has to cross between parts.
Inputs may be any that keep to these rules, and one draw needn't show every extreme that they name: `lengths`: every example has at least 128 real tokens, and some example of each draw has 512. Each row is a permutation; index i of fsdp holds block s % 4 of example s // 4, s = layout[m, i]. `hadamard_rows`: each row is a permutation. `entry_pick`: row 0 indexes the row-major 1024 x 128 grid_a, row 1 the row-major 128 x 1024 grid_b.
All inputs are finite; a program needn't handle non-finite values.
Results may differ from a plain program's by a relative error of at most 0.0003.
Values may be sent and summed in bfloat16 or wider, within the bound.
A program may use at most 64 MiB of HBM per device.

v0:
```python
import math

import jax
import jax.numpy as jnp
from jax import lax
from jax.sharding import PartitionSpec as P

K = 8192
CAND = 1024
EX_LEN = 512


def bit_parity(values):
    counted = jnp.zeros_like(values)
    for shift_amount in range(16):
        counted = counted + jnp.bitwise_and(jnp.right_shift(values, shift_amount), 1)
    return jnp.bitwise_and(counted, 1)


def parity_table(left_bits, right_bits):
    anded = jnp.bitwise_and(left_bits[:, None], right_bits[None, :])
    return 1 - 2 * bit_parity(anded)


def project_rows(inputs, rows_chosen):
    tok_count, feature_width = inputs.shape
    low_size = min(feature_width, 1024)
    high_count = feature_width // low_size
    low_bits = jnp.arange(low_size, dtype=jnp.int32)
    base_table = parity_table(low_bits, rows_chosen).astype(jnp.bfloat16)
    high_bits = jnp.arange(high_count, dtype=jnp.int32) * low_size
    signs_high = parity_table(high_bits, rows_chosen).astype(jnp.float32)
    pieces = inputs.reshape(tok_count, high_count, low_size)
    partial_value = jnp.einsum(
        "thd,dk->thk", pieces, base_table, preferred_element_type=jnp.float32
    )
    return jnp.sum(partial_value * signs_high[None, :, :], axis=1) / math.sqrt(feature_width)


def rank_mix(values, signs):
    rank_size = values.shape[1]
    rank_bits = jnp.arange(rank_size, dtype=jnp.int32)
    table = parity_table(rank_bits, rank_bits).astype(jnp.float32)
    mixed = jnp.dot(
        values * signs, table, precision=lax.Precision.HIGHEST, preferred_element_type=jnp.float32
    )
    return mixed / math.sqrt(rank_size)


def per_device(
    activations,
    cotangent,
    adapter,
    lengths,
    layout,
    feature_signs,
    rank_signs,
    hadamard_rows,
    entry_pick,
    val_feats,
):
    micro_index = lax.axis_index("batch")
    member = lax.axis_index("fsdp")
    tok_count = activations.shape[1]
    block_count = EX_LEN // tok_count
    example_total = lengths.shape[1]
    slot_row = lax.dynamic_index_in_dim(layout, micro_index, 0, keepdims=False)
    my_slot = lax.dynamic_index_in_dim(slot_row, member, 0, keepdims=False)
    my_example = my_slot // block_count
    length_row = lax.dynamic_index_in_dim(lengths, micro_index, 0, keepdims=False)
    my_length = lax.dynamic_index_in_dim(length_row, my_example, 0, keepdims=False)
    position = my_slot % block_count * tok_count + jnp.arange(tok_count, dtype=jnp.int32)
    weight = (position < my_length).astype(jnp.float32)[:, None]
    inputs = activations[0]
    grads = cotangent[0]
    piece = lax.all_gather(adapter, "fsdp", axis=1, tiled=True)
    reduced = jnp.dot(inputs, piece[0], preferred_element_type=jnp.float32)
    backward = jnp.dot(grads, piece[1], preferred_element_type=jnp.float32)
    signs_in = (1 - 2 * feature_signs[0]).astype(jnp.bfloat16)
    signs_out = (1 - 2 * feature_signs[1]).astype(jnp.bfloat16)
    rank_a = (1 - 2 * rank_signs[0]).astype(jnp.float32)
    rank_b = (1 - 2 * rank_signs[1]).astype(jnp.float32)
    left_a = project_rows(inputs * signs_in[None, :], hadamard_rows[0, :CAND])
    right_b = project_rows(grads * signs_out[None, :], hadamard_rows[1, :CAND])
    right_a = rank_mix(backward, rank_a) * weight
    left_b = rank_mix(reduced, rank_b) * weight
    grid_a = jnp.dot(
        left_a.T, right_a, precision=lax.Precision.HIGHEST, preferred_element_type=jnp.float32
    )
    grid_b = jnp.dot(
        left_b.T, right_b, precision=lax.Precision.HIGHEST, preferred_element_type=jnp.float32
    )
    partial_feats = jnp.concatenate(
        [grid_a.reshape(-1)[entry_pick[0]], grid_b.reshape(-1)[entry_pick[1]]]
    )
    example_ids = jnp.arange(example_total, dtype=jnp.int32)
    mine = (example_ids == my_example).astype(jnp.float32)
    term = mine[:, None] * partial_feats[None, :]
    feat_slice = lax.psum_scatter(term, "fsdp", scatter_dimension=1, tiled=True)
    dots = jnp.dot(
        feat_slice, val_feats.T, precision=lax.Precision.HIGHEST, preferred_element_type=jnp.float32
    )
    feat_sq = jnp.sum(feat_slice * feat_slice, axis=1)
    val_sq = jnp.sum(val_feats * val_feats, axis=1)
    dots, feat_sq, val_sq = lax.psum((dots, feat_sq, val_sq), "fsdp")
    similarity = (
        math.sqrt(K)
        * dots
        * lax.rsqrt(feat_sq[:, None] + 1e-06)
        * lax.rsqrt(val_sq[None, :] + 1e-06)
    )
    return similarity[None]


def solution(mesh):
    return jax.shard_map(
        per_device,
        mesh=mesh,
        in_specs=(
            P("batch", ("groups", "fsdp"), None),
            P("batch", ("groups", "fsdp"), None),
            P(None, "fsdp", None),
            P(None, "groups"),
            P(None, "groups"),
            P(),
            P(),
            P(),
            P(),
            P("groups", "fsdp"),
        ),
        out_specs=P("batch", "groups", None),
        check_vma=False,
    )
```

profile of v0, /device:TPU:0, one launch (start us, length us, event | category | flops | bytes accessed | tf_op | source)
XLA Modules:
  0.0 259.1 jit_solution(13391417947686875107)
XLA Ops:
  6.5 0.0 all-gather.2.cloned.1.call-start
  6.5 0.7 all-gather.2.cloned.1.call-update
  7.3 0.0 reduce-scatter.4.cloned.1.call-start
  7.3 1.3 dynamic_slice.12
  11.2 1.1 convert_reduce_fusion.1
  12.4 0.0 copy-start.1
  12.4 0.0 copy-start.6
  12.4 0.0 copy-start.5
  12.4 0.0 copy-start.4
  12.4 4.5 %copy.14 = bf16[16,8,8,1024]{3,2,1,0:T(8,128)(2,1)} copy(bf16[16,8,8,1024]{3,1,2,0:T(8,128)(2,1)} %bitcast.69) | data formatting | bytes 4194304
  16.9 0.0 copy-done.1
  16.9 1.4 copy.13
  18.3 0.0 copy-done.6
  18.3 0.6 dynamic_slice.13
  18.9 0.7 compare_select_fusion.2
  19.6 0.0 copy-done.5
  19.6 0.8 fusion.192
  20.4 0.0 copy-done.4
  20.5 0.2 fusion.87
  20.7 1.9 bitcast_multiply_fusion
  22.5 0.3 bitcast_multiply_fusion.1
  22.8 10.3 %multiply_reduce_fusion = f32[128,1024]{1,0:T(8,128)S(1)} fusion(bf16[128,8,1024]{2,1,0:T(8,128)(2,1)S(1)} %bitcast_multiply_fusion, f32[8,1024]{1,0:T(8,128)S(1)} %get-tuple-element.17, s32[1024]{0:T(1024)S(1)} %bitcast.76), kind=kOutput, calls=%fused_computation.3 | convolution fusion | flops 2203975680 | bytes 2658304 | tf_op jit(solution)/shard_map/thd,dk->thk/dot_general | solution.py:34
  33.1 0.0 copy-start.2
  33.1 10.1 %multiply_reduce_fusion.1 = f32[128,1024]{1,0:T(8,128)S(1)} fusion(bf16[128,8,1024]{2,1,0:T(8,128)(2,1)S(1)} %bitcast_multiply_fusion.1, f32[8,1024]{1,0:T(8,128)S(1)} %get-tuple-element.16, s32[1024]{0:T(1024)S(1)} %bitcast.74), kind=kOutput, calls=%fused_computation.5 | convolution fusion | flops 2203975680 | bytes 2658304 | tf_op jit(solution)/shard_map/thd,dk->thk/dot_general | solution.py:34
  43.2 42.4 %all-gather.2.cloned.1.call-done = bf16[2,8192,128]{2,1,0:T(8,128)(2,1)} async-done(((bf16[2,1024,128]{2,1,0:T(8,128)(2,1)}), bf16[2,8192,128]{2,1,0:T(8,128)(2,1)}) %all-gather.2.cloned.1.call-update) | async-done | bytes 4194320 | tf_op jit(solution)/shard_map/all_gather | solution.py:76
  85.7 0.0 copy-start.3
  85.7 0.0 copy-done.2
  85.7 2.4 fusion.45
  88.1 0.3 convolution_multiply_fusion
  88.5 0.0 copy-done.3
  88.5 2.3 fusion.42
  90.8 0.3 convolution_multiply_fusion.1
  91.1 0.6 convolution_bitcast_fusion.1
  91.8 0.1 copy.15
  91.9 23.0 %gather_fusion.1 = f32[4096]{0:T(1024)S(1)} fusion(f32[131072]{0:T(1024)S(1)} %bitcast.66, s32[4096]{0:T(1024)S(1)} %broadcast_clamp_fusion), kind=kCustom, calls=%fused_computation.1 | custom fusion | bytes 49152 | tf_op jit(solution)/shard_map/gather | solution.py:94
  114.9 1.0 convolution_bitcast_fusion
  115.9 23.0 %gather_fusion = f32[4096]{0:T(1024)S(1)} fusion(f32[131072]{0:T(1024)S(1)} %convolution_bitcast_fusion, s32[4096]{0:T(1024)S(1)} %broadcast_clamp_fusion.1), kind=kCustom, calls=%fused_computation | custom fusion | bytes 49152 | tf_op jit(solution)/shard_map/gather | solution.py:94
  139.0 0.1 broadcast_multiply_fusion
  139.1 0.0 copy-start
  139.1 2.6 %copy.11 = f32[2,8192]{0,1:T(8,128)} copy(f32[2,8192]{1,0:T(2,128)S(1)} %broadcast_multiply_fusion) | data formatting | bytes 131072
  141.7 0.0 reduce-scatter.4.cloned.1.call-update
  141.7 0.0 copy-done
  141.7 0.1 multiply_reduce_fusion.2
  141.9 86.2 %reduce-scatter.4.cloned.1.call-done = f32[1024,2]{1,0:T(8,128)} async-done(((f32[8192,2]{1,0:T(8,128)}), f32[1024,2]{1,0:T(8,128)}) %reduce-scatter.4.cloned.1.call-update) | async-done | bytes 8208
  228.1 1.2 copy.12
  229.3 0.1 multiply_reduce_fusion.3
  229.4 2.0 fusion.124
  231.4 20.2 %all-reduce = (f32[2,256]{1,0:T(2,128)S(1)}, f32[2]{0:T(128)S(1)}, f32[256]{0:T(256)S(1)}) all-reduce(f32[2,256]{1,0:T(2,128)S(1)} %fusion.124, f32[2]{0:T(128)S(1)} %multiply_reduce_fusion.3, f32[256]{0:T(256)S(1)} %multiply_reduce_fusion.2), channel_id=1, replica_groups=mesh['groups'=2,'fsdp'=8,'batch'=2] {'fsdp'}, use_global_device_ids=true, to_apply=%region_3.4 | all-reduce | flops 770 | bytes 6160 | tf_op jit(solution)/shard_map/psum | solution.py:105
  251.6 0.7 multiply_bitcast_fusion
  (11 shorter events, 0.1 us)
Async XLA Ops:
  6.5 79.2 %all-gather.2.cloned.1.call-start = ((), (), s32[]{:S(2)}) async-start(), calls=%async_computation.1 | async-start | bytes 4718592 | tf_op jit(solution)/shard_map/all_gather | solution.py:76
  7.3 220.8 %reduce-scatter.4.cloned.1.call-start = ((), (), s32[]{:S(2)}) async-start(), calls=%async_computation.2 | async-start | bytes 4718592
  12.4 4.5 %copy-start.1 = (bf16[1,128,8192]{2,1,0:T(8,128)(2,1)S(1)}, bf16[1,128,8192]{2,1,0:T(8,128)(2,1)}, u32[]{:S(2)}) copy-start(bf16[1,128,8192]{2,1,0:T(8,128)(2,1)} %param.10) | copy-start | bytes 6291460
  12.4 5.9 %copy-start.6 = (s32[2,2]{1,0:T(2,128)S(1)}, s32[2,2]{1,0:T(2,128)}, u32[]{:S(2)}) copy-start(s32[2,2]{1,0:T(2,128)} %param.13) | copy-start | bytes 52
  12.4 7.2 %copy-start.5 = (s32[2,128]{1,0:T(2,128)S(1)}, s32[2,128]{1,0:T(2,128)}, u32[]{:S(2)}) copy-start(s32[2,128]{1,0:T(2,128)} %param.16) | copy-start | bytes 3076
  12.4 8.0 %copy-start.4 = (s32[2,4096]{1,0:T(2,128)S(1)}, s32[2,4096]{1,0:T(2,128)}, u32[]{:S(2)}) copy-start(s32[2,4096]{1,0:T(2,128)} %param.18) | copy-start | bytes 98308
  33.1 52.6 %copy-start.2 = (bf16[1,128,8192]{2,1,0:T(8,128)(2,1)S(1)}, bf16[1,128,8192]{2,1,0:T(8,128)(2,1)}, u32[]{:S(2)}) copy-start(bf16[1,128,8192]{2,1,0:T(8,128)(2,1)} %param.10) | copy-start | bytes 6291460
  85.7 2.8 %copy-start.3 = (bf16[1,128,8192]{2,1,0:T(8,128)(2,1)S(1)}, bf16[1,128,8192]{2,1,0:T(8,128)(2,1)}, u32[]{:S(2)}) copy-start(bf16[1,128,8192]{2,1,0:T(8,128)(2,1)} %param.11) | copy-start | bytes 6291460
  139.1 2.7 %copy-start = (f32[256,1024]{1,0:T(8,128)S(1)}, f32[256,1024]{1,0:T(8,128)}, u32[]{:S(2)}) copy-start(f32[256,1024]{1,0:T(8,128)} %param.19) | copy-start | bytes 3145732
Sparse Core Ops, SparseCore 0:
  9.5 76.1 all-gather.1
  141.8 86.2 reduce-scatter.3
where the time goes:
time: 260 us; the launch traced here: 259 us
  waiting for transfers between devices  129 us (50%)
  local copies, waits for them, and re-layouts  58.6 us (23%)
  matrix products  29.4 us (11%)
  blocking collectives  20.2 us (8%)
  between operations  16.3 us (6%)
  other arithmetic  5.23 us (2%)
    unnamed x3, waiting for transfers between devices  86.9 us
    all_gather x1, waiting for transfers between devices, per_device(): piece = lax.all_gather(adapter, 'fsdp', axis=1, tiled=True)  42.4 us
    gather x1, local copies, waits for them, and re-layouts, per_device(): grid_b.reshape(-1)[entry_pick[1]]  23 us
    gather x1, local copies, waits for them, and re-layouts, per_device(): grid_a.reshape(-1)[entry_pick[0]]  23 us
    dot_general x2, matrix products, project_rows(): jnp.einsum('thd,dk->thk', pieces, base_table, preferred_element_type=jnp....  20.4 us
    psum x1, blocking collectives, per_device(): dots, feat_sq, val_sq = lax.psum((dots, feat_sq, val_sq), 'fsdp')  20.2 us
    unnamed x19, local copies, waits for them, and re-layouts  9.85 us
  transfers between devices with their start and end apart: 2, of which 2 were waited for; matrix products, arithmetic and copies ran while one was open for 13% of the time, Pallas kernels for 0%

commit v1 on v0

--- a/solution.py
+++ b/solution.py
@@ -3,6 +3,8 @@
 import jax
 import jax.numpy as jnp
 from jax import lax
+from jax.experimental import pallas as pl
+from jax.experimental.pallas import tpu as pltpu
 from jax.sharding import PartitionSpec as P
 
 K = 8192
@@ -47,7 +49,7 @@
     return mixed / math.sqrt(rank_size)
 
 
-def per_device(
+def per_device_any_size(
     activations,
     cotangent,
     adapter,
@@ -112,9 +114,431 @@
     return similarity[None]
 
 
+MESH = pl.DeviceIdType.MESH
+F32 = jnp.float32
+BF16 = jnp.bfloat16
+D_MODEL = 8192
+RANK = 128
+LOW = 1024
+HIGH = D_MODEL // LOW
+TOK = 128
+MEMBERS = 8
+SHARD = D_MODEL // MEMBERS
+HALF = K // 2
+VALS = 256
+SLICE = K // MEMBERS
+PLANE_ROWS = 640
+CROSS_ROWS = SHARD - PLANE_ROWS
+
+
+def sign_rows(row, bit):
+    signs = (1 - 2 * jnp.bitwise_and(jnp.right_shift(row, bit), 1)).astype(F32)
+    return jnp.broadcast_to(signs, (16, row.shape[1])).astype(BF16)
+
+
+def fill_signs(table_ref, row, bits):
+    width = row.shape[1]
+    index = lax.broadcasted_iota(jnp.int32, (16, width), 0)
+    both = jnp.bitwise_and(index, jnp.broadcast_to(row, (16, width)))
+    both = jnp.bitwise_xor(both, jnp.right_shift(both, 2))
+    both = jnp.bitwise_xor(both, jnp.right_shift(both, 1))
+    table_ref[0:16, :] = (1 - 2 * jnp.bitwise_and(both, 1)).astype(F32).astype(BF16)
+    for bit in range(4, bits):
+        flip = sign_rows(row, bit)
+        span = 1 << bit
+        for at in range(0, span, 16):
+            table_ref[span + at : span + at + 16, :] = table_ref[at : at + 16, :] * flip
+
+
+def split_rows(values):
+    top = values.astype(BF16)
+    rest = (values - top.astype(F32)).astype(BF16)
+    return jnp.concatenate([top, rest], axis=0)
+
+
+def dot_t(left, right):
+    return lax.dot_general(
+        left, right, (((1,), (1,)), ((), ())), preferred_element_type=F32
+    )
+
+
+def kernel(
+    lengths_ref,
+    layout_ref,
+    signs_ref,
+    rank_ref,
+    rows_ref,
+    pick_ref,
+    act_hbm,
+    cot_hbm,
+    adapter_hbm,
+    val_hbm,
+    out_ref,
+    act_ref,
+    cot_ref,
+    val_ref,
+    gathered,
+    x_ref,
+    t_ref,
+    left_ref,
+    sel_a,
+    sel_b,
+    mix_a,
+    mix_b,
+    val_parts,
+    val_sq,
+    feat_out,
+    feat_in,
+    dots_out,
+    dots_in,
+    local_sem,
+    z_send,
+    z_recv,
+    x_send,
+    x_recv,
+    y_send,
+    y_recv,
+    ca_send,
+    ca_recv,
+    cb_send,
+    cb_recv,
+    f_send,
+    f_recv,
+    d_send,
+    d_recv,
+):
+    group = lax.axis_index("groups")
+    member = lax.axis_index("fsdp")
+    core = lax.axis_index("batch")
+    col = member % 2
+    depth = member // 2
+    mates = [
+        depth,
+        depth + 1 - 2 * (depth % 2),
+        (depth + 2) % 4,
+        3 - depth,
+    ]
+    other_group = {"groups": 1 - group}
+    other_core = {"batch": 1 - core}
+    across = {"fsdp": depth * 2 + 1 - col}
+
+    loads = [
+        pltpu.make_async_copy(act_hbm.at[0], act_ref, local_sem.at[0]),
+        pltpu.make_async_copy(cot_hbm.at[0], cot_ref, local_sem.at[1]),
+        pltpu.make_async_copy(val_hbm, val_ref, local_sem.at[2]),
+        pltpu.make_async_copy(adapter_hbm.at[0], gathered.at[0, member], local_sem.at[3]),
+        pltpu.make_async_copy(adapter_hbm.at[1], gathered.at[1, member], local_sem.at[4]),
+    ]
+    for load in loads:
+        load.start()
+
+    barrier = pltpu.get_barrier_semaphore()
+    for step in range(1, MEMBERS):
+        pl.semaphore_signal(
+            barrier, inc=1, device_id={"fsdp": (member + step) % MEMBERS}, device_id_type=MESH
+        )
+    pl.semaphore_signal(barrier, inc=1, device_id=other_group, device_id_type=MESH)
+    pl.semaphore_signal(barrier, inc=1, device_id=other_core, device_id_type=MESH)
+    pl.semaphore_wait(barrier, MEMBERS + 1)
+
+    plane = pl.ds(pl.multiple_of(group * CROSS_ROWS, 128), PLANE_ROWS)
+    cross_out = pl.ds(pl.multiple_of(group * PLANE_ROWS, 128), CROSS_ROWS)
+    cross_in = pl.ds(pl.multiple_of((1 - group) * PLANE_ROWS, 128), CROSS_ROWS)
+    own = adapter_hbm.at[core, plane]
+
+    def remote(src, dst, send, recv, where):
+        return pltpu.make_async_remote_copy(
+            src_ref=src,
+            dst_ref=dst,
+            send_sem=send,
+            recv_sem=recv,
+            device_id=where,
+            device_id_type=MESH,
+        )
+
+    sent = []
+
+    def go(copy):
+        copy.start()
+        sent.append(copy)
+
+    home = gathered.at[core, member, plane]
+    go(remote(own, home, x_send.at[0], x_recv.at[0], across))
+    for k in (3, 2, 1):
+        go(remote(own, home, z_send.at[k], z_recv.at[k], {"fsdp": mates[k] * 2 + col}))
+
+    order = [("x", 0), ("z", 1), ("x", 1), ("z", 3), ("x", 3), ("z", 2), ("x", 2)]
+    shard_of = [
+        mates[k] * 2 + (col if kind == "z" else 1 - col) for kind, k in order
+    ]
+
+    def receive(place):
+        kind, k = order[place]
+        shard = shard_of[place]
+        block = gathered.at[core, shard, plane]
+        sems = (z_send, z_recv) if kind == "z" else (x_send, x_recv)
+        remote(block, block, sems[0].at[k], sems[1].at[k], across).wait_recv()
+        if kind == "z":
+            go(remote(block, block, x_send.at[k], x_recv.at[k], across))
+        part = gathered.at[core, shard, cross_out]
+        go(remote(part, part, y_send.at[place], y_recv.at[place], other_group))
+        go(remote(block, block, ca_send.at[place], ca_recv.at[place], other_core))
+
+    def receive_cross(place):
+        part = gathered.at[core, shard_of[place], cross_in]
+        remote(part, part, y_send.at[place], y_recv.at[place], other_group).wait_recv()
+        go(remote(part, part, cb_send.at[place], cb_recv.at[place], other_core))
+
+    def receive_core(place):
+        block = gathered.at[1 - core, shard_of[place], plane]
+        part = gathered.at[1 - core, shard_of[place], cross_in]
+        remote(block, block, ca_send.at[place], ca_recv.at[place], other_core).wait_recv()
+        remote(part, part, cb_send.at[place], cb_recv.at[place], other_core).wait_recv()
+
+    def fill_inputs(which, in_ref):
+        for high in range(HIGH):
+            lanes = slice(high * LOW, (high + 1) * LOW)
+            flip = sign_rows(signs_ref[which : which + 1, lanes], 0)
+            for at in range(0, TOK, 16):
+                x_ref[high * TOK + at : high * TOK + at + 16, :] = (
+                    in_ref[at : at + 16, lanes] * flip
+                )
+
+    def project(which):
+        def tile(n, carry):
+            lanes = pl.ds(pl.multiple_of(n * 256, 256), 256)
+            parts = jnp.dot(x_ref[...], t_ref[:, lanes], preferred_element_type=F32)
+            row = rows_ref[which : which + 1, lanes]
+            level = [parts[h * TOK : (h + 1) * TOK] for h in range(HIGH)]
+            for bit in range(10, 13):
+                flip = (1 - 2 * jnp.bitwise_and(jnp.right_shift(row, bit), 1)).astype(F32)
+                level = [
+                    level[2 * i] + level[2 * i + 1] * flip for i in range(len(level) // 2)
+                ]
+            left_ref[:, lanes] = split_rows(level[0])
+            return carry
+
+        lax.fori_loop(0, CAND // 256, tile, 0)
+
+    def row_index(which, lanes):
+        picked = pick_ref[which : which + 1, lanes]
+        if which == 0:
+            return jnp.right_shift(picked, 7)
+        return jnp.bitwise_and(picked, CAND - 1)
+
+    def rank_index(which):
+        picked = pick_ref[which : which + 1, :]
+        if which == 0:
+            return jnp.bitwise_and(picked, RANK - 1)
+        return jnp.right_shift(picked, 10)
+
+    def select(which, sel_ref, begin, end):
+        def tile(n, carry):
+            lanes = pl.ds(pl.multiple_of(n * 256, 256), 256)
+            wanted = row_index(which, lanes)
+            index = lax.broadcasted_iota(jnp.int32, (CAND, 256), 0)
+            hot = jnp.where(index == wanted, 1.0, 0.0).astype(BF16)
+            both = jnp.dot(left_ref[...], hot, preferred_element_type=F32)
+            sel_ref[:, lanes] = both[:TOK] + both[TOK:]
+            return carry
+
+        lax.fori_loop(begin, end, tile, 0)
+
+    def prepare_scores():
+        values = val_ref[...]
+        val_parts[...] = split_rows(values)
+        squares = split_rows(values * values)
+        sums = dot_t(jnp.ones((16, SLICE), BF16), squares)
+        val_sq[...] = sums[0:8, :VALS] + sums[0:8, VALS:]
+
+    loads[0].wait()
+    fill_signs(t_ref, rows_ref[0:1, 0:CAND], 10)
+    fill_inputs(0, act_ref)
+    project(0)
+    receive(0)
+    receive(1)
+    select(0, sel_a, 0, 8)
+    receive(2)
+    select(0, sel_a, 8, 16)
+    receive(3)
+    receive_cross(0)
+    receive_cross(1)
+    loads[1].wait()
+    fill_signs(t_ref, rows_ref[1:2, 0:CAND], 10)
+    fill_inputs(1, cot_ref)
+    receive(4)
+    receive_cross(2)
+    project(1)
+    receive(5)
+    receive_cross(3)
+    select(1, sel_b, 0, 8)
+    receive(6)
+    receive_cross(4)
+    select(1, sel_b, 8, 16)
+    receive_cross(5)
+    fill_signs(mix_a, rank_index(0), 7)
+    fill_signs(mix_b, rank_index(1), 7)
+    receive_cross(6)
+    loads[2].wait()
+    prepare_scores()
+    loads[3].wait()
+    loads[4].wait()
+
+    def both_products(shard):
+        lanes = pl.ds(pl.multiple_of(shard * SHARD, SHARD), SHARD)
+        return (
+            jnp.dot(act_ref[:, lanes], gathered[0, shard], preferred_element_type=F32),
+            jnp.dot(cot_ref[:, lanes], gathered[1, shard], preferred_element_type=F32),
+        )
+
+    reduced, backward = both_products(member)
+    for place in range(MEMBERS - 1):
+        receive_core(place)
+        more_r, more_b = both_products(shard_of[place])
+        reduced = reduced + more_r
+        backward = backward + more_b
+
+    slot = layout_ref[core, member]
+    blocks = EX_LEN // TOK
+    example = slot // blocks
+    length = jnp.int32(0)
+    for e in range(lengths_ref.shape[1]):
+        length = jnp.where(example == e, lengths_ref[core, e], length)
+    position = slot % blocks * TOK + lax.broadcasted_iota(jnp.int32, (TOK, RANK), 0)
+    weight = jnp.where(position < length, 1.0, 0.0)
+    rank_flip = (1 - 2 * rank_ref[...]).astype(F32)
+    mixed_a = split_rows(backward * rank_flip[0:1] * weight)
+    mixed_b = split_rows(reduced * rank_flip[1:2] * weight)
+    scale = 1.0 / math.sqrt(D_MODEL * RANK)
+    for n in range(MEMBERS):
+        mixed, mix, sel = (mixed_a, mix_a, sel_a) if n < MEMBERS // 2 else (mixed_b, mix_b, sel_b)
+        lanes = slice(n % (MEMBERS // 2) * SLICE, (n % (MEMBERS // 2) + 1) * SLICE)
+        both = jnp.dot(mixed, mix[:, lanes], preferred_element_type=F32)
+        terms = sel[:, lanes] * (both[:TOK] + both[TOK:])
+        feat_out[n] = jnp.sum(terms, axis=0, keepdims=True) * scale
+
+    feat_in[member] = feat_out[member]
+    for step in range(1, MEMBERS):
+        to = (member + step) % MEMBERS
+        go(
+            remote(
+                feat_out.at[to], feat_in.at[member], f_send.at[step], f_recv.at[step], {"fsdp": to}
+            )
+        )
+    for step in range(1, MEMBERS):
+        source = (member + MEMBERS - step) % MEMBERS
+        remote(
+            feat_out.at[source], feat_in.at[source], f_send.at[step], f_recv.at[step],
+            {"fsdp": source},
+        ).wait_recv()
+
+    examples = lengths_ref.shape[1]
+    totals = [jnp.zeros((1, SLICE), F32) for _ in range(examples)]
+    for n in range(MEMBERS):
+        owner = layout_ref[core, n] // blocks
+        piece = feat_in[n]
+        for e in range(examples):
+            totals[e] = totals[e] + piece * jnp.where(owner == e, 1.0, 0.0)
+    row_at = lax.broadcasted_iota(jnp.int32, (8, SLICE), 0)
+    feats = jnp.zeros((8, SLICE), F32)
+    for e in range(examples):
+        feats = jnp.where(row_at == e, jnp.broadcast_to(totals[e], (8, SLICE)), feats)
+    products = dot_t(split_rows(feats), val_parts[...])
+    dots = products[0:8, :VALS] + (products[8:16, :VALS] + products[0:8, VALS:])
+    feat_sq = jnp.sum(feats * feats, axis=1, keepdims=True)
+    at = lax.broadcasted_iota(jnp.int32, (8, VALS), 0)
+    dots_out[:, 0:VALS] = jnp.where(at == examples, val_sq[...], dots)
+    dots_out[:, VALS:] = jnp.broadcast_to(feat_sq, (8, RANK))
+    dots_in[member] = dots_out[...]
+    for step in range(1, MEMBERS):
+        to = (member + step) % MEMBERS
+        go(remote(dots_out, dots_in.at[member], d_send.at[step], d_recv.at[step], {"fsdp": to}))
+    for step in range(1, MEMBERS):
+        source = (member + MEMBERS - step) % MEMBERS
+        remote(
+            dots_out, dots_in.at[source], d_send.at[step], d_recv.at[step], {"fsdp": source}
+        ).wait_recv()
+    total = dots_in[0]
+    for n in range(1, MEMBERS):
+        total = total + dots_in[n]
+    out_ref[0] = (
+        math.sqrt(K)
+        * total[0:examples, 0:VALS]
+        * lax.rsqrt(total[0:examples, VALS : VALS + 1] + 1e-06)
+        * lax.rsqrt(total[examples : examples + 1, 0:VALS] + 1e-06)
+    )
+    for copy in sent:
+        copy.wait_send()
+
+
+def per_device(
+    activations,
+    cotangent,
+    adapter,
+    lengths,
+    layout,
+    feature_signs,
+    rank_signs,
+    hadamard_rows,
+    entry_pick,
+    val_feats,
+):
+    examples = lengths.shape[1]
+    smem = pl.BlockSpec(memory_space=pltpu.SMEM)
+    vmem = pl.BlockSpec(memory_space=pltpu.VMEM)
+    hbm = pl.BlockSpec(memory_space=pl.ANY)
+    dma = pltpu.SemaphoreType.DMA
+    return pl.pallas_call(
+        kernel,
+        out_shape=jax.ShapeDtypeStruct((1, examples, VALS), F32),
+        in_specs=[smem] * 2 + [vmem] * 4 + [hbm] * 4,
+        out_specs=vmem,
+        scratch_shapes=[
+            pltpu.VMEM((TOK, D_MODEL), BF16),
+            pltpu.VMEM((TOK, D_MODEL), BF16),
+            pltpu.VMEM((VALS, SLICE), F32),
+            pltpu.VMEM((2, MEMBERS, SHARD, RANK), BF16),
+            pltpu.VMEM((HIGH * TOK, LOW), BF16),
+            pltpu.VMEM((LOW, CAND), BF16),
+            pltpu.VMEM((2 * TOK, CAND), BF16),
+            pltpu.VMEM((TOK, HALF), F32),
+            pltpu.VMEM((TOK, HALF), F32),
+            pltpu.VMEM((RANK, HALF), BF16),
+            pltpu.VMEM((RANK, HALF), BF16),
+            pltpu.VMEM((2 * VALS, SLICE), BF16),
+            pltpu.VMEM((8, VALS), F32),
+            pltpu.VMEM((MEMBERS, 1, SLICE), F32),
+            pltpu.VMEM((MEMBERS, 1, SLICE), F32),
+            pltpu.VMEM((8, VALS + RANK), F32),
+            pltpu.VMEM((MEMBERS, 8, VALS + RANK), F32),
+            dma((5,)),
+        ]
+        + [dma((4,))] * 4
+        + [dma((MEMBERS,))] * 10,
+        compiler_params=pltpu.CompilerParams(
+            collective_id=0, has_side_effects=True, vmem_limit_bytes=48 * 1024 * 1024
+        ),
+        cost_estimate=pl.CostEstimate(
+            flops=10_000_000_000, bytes_accessed=8_000_000, transcendentals=0
+        ),
+    )(
+        lengths,
+        layout,
+        feature_signs,
+        rank_signs,
+        hadamard_rows,
+        entry_pick,
+        activations,
+        cotangent,
+        adapter,
+        val_feats,
+    )
+
+
 def solution(mesh):
+    fits = mesh.shape["fsdp"] == MEMBERS and mesh.shape["batch"] == 2 and mesh.shape["groups"] == 2
     return jax.shard_map(
-        per_device,
+        per_device if fits else per_device_any_size,
         mesh=mesh,
         in_specs=(
             P("batch", ("groups", "fsdp"), None),

time: 260 us -> 65.7 us (0.25)
  waiting for transfers between devices: 129 us -> 0 us
  Pallas kernels: 0 us -> 54.7 us
  local copies, waits for them, and re-layouts: 58.6 us -> 10.5 us
  matrix products: 29.4 us -> 0 us
  blocking collectives: 20.2 us -> 0 us
  between operations: 16.3 us -> 0.02 us
  other arithmetic: 5.23 us -> 0 us
    unnamed x3 -> x0, waiting for transfers between devices: 86.9 us -> none
    pallas_call x0 -> x1, Pallas kernels: none -> 54.7 us  [per_device(): pl.pallas_call(kernel, out_shape=jax.ShapeDtypeStruct((1, examples, VALS)...]
    gather x2 -> x0, local copies, waits for them, and re-layouts: 46.1 us -> none  [the longest x1 23 us: per_device(): grid_b.reshape(-1)[entry_pick[1]]]
    all_gather x1 -> x0, waiting for transfers between devices: 42.4 us -> none  [per_device(): piece = lax.all_gather(adapter, 'fsdp', axis=1, tiled=True)]
    dot_general x9 -> x0, matrix products: 29.4 us -> none  [the longest x2 20.4 us: project_rows(): jnp.einsum('thd,dk->thk', pieces, base_table, preferred_element_type=jnp....]
    psum x1 -> x0, blocking collectives: 20.2 us -> none  [per_device(): dots, feat_sq, val_sq = lax.psum((dots, feat_sq, val_sq), 'fsdp')]
    mul x7 -> x0, other arithmetic: 2.91 us -> none  [the longest x1 1.87 us: per_device(): right_b = project_rows(grads * signs_out[None, :], hadamard_rows[1, :CAND])]
    unnamed x19 -> x21, local copies, waits for them, and re-layouts: 9.85 us -> 10.5 us
  transfers between devices with their start and end apart: 2 -> 0, of which waited for: 2 -> 0; matrix products, arithmetic and copies ran while one was open for 13% -> 0% of each run, Pallas kernels for 0% -> 0%
where the time goes in v1:
time: 65.7 us; the launch traced here: 65.2 us
  Pallas kernels  54.7 us (83%)
  local copies, waits for them, and re-layouts  10.5 us (16%)
    pallas_call x1, Pallas kernels, per_device(): pl.pallas_call(kernel, out_shape=jax.ShapeDtypeStruct((1, examples, VALS)...  54.7 us
    unnamed x21, local copies, waits for them, and re-layouts  10.5 us

profile of v1, /device:TPU:0, one launch (start us, length us, event | category | flops | bytes accessed | tf_op | source)
XLA Modules:
  0.0 65.2 jit_solution(6267761817174329169)
XLA Ops:
  0.0 0.0 copy-start
  0.0 1.6 %copy-done = bf16[1,128,8192]{2,1,0:T(8,128)(2,1)S(1)} copy-done((bf16[1,128,8192]{2,1,0:T(8,128)(2,1)S(1)}, bf16[1,128,8192]{2,1,0:T(8,128)(2,1)}, u32[]{:S(2)}) %copy-start) | copy-done | bytes 2097176
  1.6 0.0 copy-start.1
  1.6 1.6 %copy-done.1 = bf16[1,128,8192]{2,1,0:T(8,128)(2,1)S(1)} copy-done((bf16[1,128,8192]{2,1,0:T(8,128)(2,1)S(1)}, bf16[1,128,8192]{2,1,0:T(8,128)(2,1)}, u32[]{:S(2)}) %copy-start.1) | copy-done | bytes 2097176
  3.2 0.0 copy-start.2
  3.2 1.2 %copy-done.2 = f32[256,1024]{1,0:T(8,128)S(1)} copy-done((f32[256,1024]{1,0:T(8,128)S(1)}, f32[256,1024]{1,0:T(8,128)}, u32[]{:S(2)}) %copy-start.2) | copy-done | bytes 1048600
  4.4 0.0 copy-start.3
  4.4 1.0 %copy-done.3 = bf16[2,1024,128]{2,1,0:T(8,128)(2,1)S(1)} copy-done((bf16[2,1024,128]{2,1,0:T(8,128)(2,1)S(1)}, bf16[2,1024,128]{2,1,0:T(8,128)(2,1)}, u32[]{:S(2)}) %copy-start.3) | copy-done | bytes 524312
  5.5 0.0 copy-start.4
  5.5 0.8 %copy-done.4 = s32[2,8192]{1,0:T(2,128)S(1)} copy-done((s32[2,8192]{1,0:T(2,128)S(1)}, s32[2,8192]{1,0:T(2,128)}, u32[]{:S(2)}) %copy-start.4) | copy-done | bytes 65560
  6.3 0.0 copy-start.5
  6.3 0.8 %copy-done.5 = s32[2,8192]{1,0:T(2,128)S(1)} copy-done((s32[2,8192]{1,0:T(2,128)S(1)}, s32[2,8192]{1,0:T(2,128)}, u32[]{:S(2)}) %copy-start.5) | copy-done | bytes 65560
  7.1 0.0 copy-start.6
  7.1 0.8 %copy-done.6 = s32[2,4096]{1,0:T(2,128)S(1)} copy-done((s32[2,4096]{1,0:T(2,128)S(1)}, s32[2,4096]{1,0:T(2,128)}, u32[]{:S(2)}) %copy-start.6) | copy-done | bytes 32792
  7.9 0.0 copy-start.7
  7.9 0.7 %copy-done.7 = s32[2,2]{1,0:T(2,128)S(1)} copy-done((s32[2,2]{1,0:T(2,128)S(1)}, s32[2,2]{1,0:T(2,128)}, u32[]{:S(2)}) %copy-start.7) | copy-done | bytes 40
  8.6 0.0 copy-start.8
  8.6 0.7 %copy-done.8 = s32[2,8]{1,0:T(2,128)S(1)} copy-done((s32[2,8]{1,0:T(2,128)S(1)}, s32[2,8]{1,0:T(2,128)}, u32[]{:S(2)}) %copy-start.8) | copy-done | bytes 88
  9.2 0.0 copy-start.9
  9.3 0.7 %copy-done.9 = s32[2,128]{1,0:T(2,128)S(1)} copy-done((s32[2,128]{1,0:T(2,128)S(1)}, s32[2,128]{1,0:T(2,128)}, u32[]{:S(2)}) %copy-start.9) | copy-done | bytes 1048
  9.9 54.7 %shard_map.100 = f32[1,2,256]{2,1,0:T(2,128)S(1)} custom-call(s32[2,2]{1,0:T(2,128)S(1)} %copy-done.7, s32[2,8]{1,0:T(2,128)S(1)} %copy-done.8, s32[2,8192]{1,0:T(2,128)S(1)} %copy-done.4, s32[2,128]{1,0:T(2,128)S(1)} %copy-done.9, s32[2,8192]{1,0:T(2,128)S(1)} %copy-done.5, s32[2,4096]{1,0:T(2,128)S(1)} %copy-done.6, bf16[1,128,8192]{2,1,0:T(8,128)(2,1)S(1)} %copy-done, ...), custom_call_target="tpu_custom_call" | custom-call | flops 10000000000 | bytes 8000000 | tf_op jit(solution)/shard_map/pallas_call | solution.py:491
  64.7 0.6 copy.12
Async XLA Ops:
  0.0 1.6 %copy-start = (bf16[1,128,8192]{2,1,0:T(8,128)(2,1)S(1)}, bf16[1,128,8192]{2,1,0:T(8,128)(2,1)}, u32[]{:S(2)}) copy-start(bf16[1,128,8192]{2,1,0:T(8,128)(2,1)} %act_hbm.1) | copy-start | bytes 6291460
  1.6 1.6 %copy-start.1 = (bf16[1,128,8192]{2,1,0:T(8,128)(2,1)S(1)}, bf16[1,128,8192]{2,1,0:T(8,128)(2,1)}, u32[]{:S(2)}) copy-start(bf16[1,128,8192]{2,1,0:T(8,128)(2,1)} %cot_hbm.1) | copy-start | bytes 6291460
  3.2 1.2 %copy-start.2 = (f32[256,1024]{1,0:T(8,128)S(1)}, f32[256,1024]{1,0:T(8,128)}, u32[]{:S(2)}) copy-start(f32[256,1024]{1,0:T(8,128)} %val_hbm.1) | copy-start | bytes 3145732
  4.4 1.0 %copy-start.3 = (bf16[2,1024,128]{2,1,0:T(8,128)(2,1)S(1)}, bf16[2,1024,128]{2,1,0:T(8,128)(2,1)}, u32[]{:S(2)}) copy-start(bf16[2,1024,128]{2,1,0:T(8,128)(2,1)} %adapter_hbm.1) | copy-start | bytes 1572868
  5.5 0.8 %copy-start.4 = (s32[2,8192]{1,0:T(2,128)S(1)}, s32[2,8192]{1,0:T(2,128)}, u32[]{:S(2)}) copy-start(s32[2,8192]{1,0:T(2,128)} %signs_ref.1) | copy-start | bytes 196612
  6.3 0.8 %copy-start.5 = (s32[2,8192]{1,0:T(2,128)S(1)}, s32[2,8192]{1,0:T(2,128)}, u32[]{:S(2)}) copy-start(s32[2,8192]{1,0:T(2,128)} %rows_ref.1) | copy-start | bytes 196612
  7.1 0.8 %copy-start.6 = (s32[2,4096]{1,0:T(2,128)S(1)}, s32[2,4096]{1,0:T(2,128)}, u32[]{:S(2)}) copy-start(s32[2,4096]{1,0:T(2,128)} %pick_ref.1) | copy-start | bytes 98308
  7.9 0.7 %copy-start.7 = (s32[2,2]{1,0:T(2,128)S(1)}, s32[2,2]{1,0:T(2,128)}, u32[]{:S(2)}) copy-start(s32[2,2]{1,0:T(2,128)} %lengths_ref.1) | copy-start | bytes 52
  8.6 0.7 %copy-start.8 = (s32[2,8]{1,0:T(2,128)S(1)}, s32[2,8]{1,0:T(2,128)}, u32[]{:S(2)}) copy-start(s32[2,8]{1,0:T(2,128)} %layout_ref.1) | copy-start | bytes 196
  9.2 0.7 %copy-start.9 = (s32[2,128]{1,0:T(2,128)S(1)}, s32[2,128]{1,0:T(2,128)}, u32[]{:S(2)}) copy-start(s32[2,128]{1,0:T(2,128)} %rank_ref.1) | copy-start | bytes 3076

commit v2 on v1

--- a/solution.py
+++ b/solution.py
@@ -163,17 +163,23 @@
 
 
 def kernel(
+    lengths_hbm,
+    layout_hbm,
+    signs_hbm,
+    rank_hbm,
+    rows_hbm,
+    pick_hbm,
+    act_hbm,
+    cot_hbm,
+    adapter_hbm,
+    val_hbm,
+    out_ref,
     lengths_ref,
     layout_ref,
     signs_ref,
     rank_ref,
     rows_ref,
     pick_ref,
-    act_hbm,
-    cot_hbm,
-    adapter_hbm,
-    val_hbm,
-    out_ref,
     act_ref,
     cot_ref,
     val_ref,
@@ -215,9 +221,10 @@
     mates = [
         depth,
         depth + 1 - 2 * (depth % 2),
-        (depth + 2) % 4,
-        3 - depth,
+        2 - depth // 2,
+        3 - 3 * (depth // 2),
     ]
+    inner = (depth + 1) // 2 % 2 == 1
     other_group = {"groups": 1 - group}
     other_core = {"batch": 1 - core}
     across = {"fsdp": depth * 2 + 1 - col}
@@ -228,8 +235,14 @@
         pltpu.make_async_copy(val_hbm, val_ref, local_sem.at[2]),
         pltpu.make_async_copy(adapter_hbm.at[0], gathered.at[0, member], local_sem.at[3]),
         pltpu.make_async_copy(adapter_hbm.at[1], gathered.at[1, member], local_sem.at[4]),
+        pltpu.make_async_copy(signs_hbm, signs_ref, local_sem.at[5]),
+        pltpu.make_async_copy(rank_hbm, rank_ref, local_sem.at[6]),
+        pltpu.make_async_copy(rows_hbm, rows_ref, local_sem.at[7]),
+        pltpu.make_async_copy(pick_hbm, pick_ref, local_sem.at[8]),
+        pltpu.make_async_copy(lengths_hbm, lengths_ref, local_sem.at[9]),
+        pltpu.make_async_copy(layout_hbm, layout_ref, local_sem.at[10]),
     ]
-    for load in loads:
+    for load in loads[5:] + loads[:5]:
         load.start()
 
     barrier = pltpu.get_barrier_semaphore()
@@ -257,17 +270,30 @@
         )
 
     sent = []
+    sent_inner = []
 
     def go(copy):
         copy.start()
         sent.append(copy)
 
+    def go_inner(shard, slot, send, to):
+        copy = remote(
+            slot, gathered.at[core, shard, plane], z_send.at[send[0]], z_recv.at[send[1]],
+            {"fsdp": mates[to] * 2 + col},
+        )
+
+        @pl.when(inner)
+        def _():
+            copy.start()
+
+        sent_inner.append(copy)
+
     home = gathered.at[core, member, plane]
     go(remote(own, home, x_send.at[0], x_recv.at[0], across))
-    for k in (3, 2, 1):
-        go(remote(own, home, z_send.at[k], z_recv.at[k], {"fsdp": mates[k] * 2 + col}))
-
-    order = [("x", 0), ("z", 1), ("x", 1), ("z", 3), ("x", 3), ("z", 2), ("x", 2)]
+    go(remote(own, home, z_send.at[1], z_recv.at[1], {"fsdp": mates[1] * 2 + col}))
+    go_inner(member, own, (2, 2), 2)
+
+    order = [("x", 0), ("z", 1), ("z", 2), ("x", 1), ("z", 3), ("x", 2), ("x", 3)]
     shard_of = [
         mates[k] * 2 + (col if kind == "z" else 1 - col) for kind, k in order
     ]
@@ -279,6 +305,10 @@
         sems = (z_send, z_recv) if kind == "z" else (x_send, x_recv)
         remote(block, block, sems[0].at[k], sems[1].at[k], across).wait_recv()
         if kind == "z":
+            if k == 1:
+                go_inner(shard, block, (3, 3), 2)
+            else:
+                go_inner(shard, block, (k + 2, k), 1)
             go(remote(block, block, x_send.at[k], x_recv.at[k], across))
         part = gathered.at[core, shard, cross_out]
         go(remote(part, part, y_send.at[place], y_recv.at[place], other_group))
@@ -304,7 +334,7 @@
                     in_ref[at : at + 16, lanes] * flip
                 )
 
-    def project(which):
+    def project(which, begin, end):
         def tile(n, carry):
             lanes = pl.ds(pl.multiple_of(n * 256, 256), 256)
             parts = jnp.dot(x_ref[...], t_ref[:, lanes], preferred_element_type=F32)
@@ -318,7 +348,7 @@
             left_ref[:, lanes] = split_rows(level[0])
             return carry
 
-        lax.fori_loop(0, CAND // 256, tile, 0)
+        lax.fori_loop(begin, end, tile, 0)
 
     def row_index(which, lanes):
         picked = pick_ref[which : which + 1, lanes]
@@ -351,34 +381,37 @@
         sums = dot_t(jnp.ones((16, SLICE), BF16), squares)
         val_sq[...] = sums[0:8, :VALS] + sums[0:8, VALS:]
 
+    for load in loads[5:]:
+        load.wait()
     loads[0].wait()
     fill_signs(t_ref, rows_ref[0:1, 0:CAND], 10)
+    receive(0)
     fill_inputs(0, act_ref)
-    project(0)
-    receive(0)
     receive(1)
-    select(0, sel_a, 0, 8)
+    project(0, 0, 2)
     receive(2)
-    select(0, sel_a, 8, 16)
+    project(0, 2, 4)
     receive(3)
     receive_cross(0)
+    select(0, sel_a, 0, 5)
+    receive(4)
     receive_cross(1)
+    select(0, sel_a, 5, 10)
+    receive(5)
+    receive_cross(2)
+    select(0, sel_a, 10, 16)
+    receive(6)
+    receive_cross(3)
     loads[1].wait()
     fill_signs(t_ref, rows_ref[1:2, 0:CAND], 10)
+    receive_cross(4)
     fill_inputs(1, cot_ref)
-    receive(4)
-    receive_cross(2)
-    project(1)
-    receive(5)
-    receive_cross(3)
-    select(1, sel_b, 0, 8)
-    receive(6)
-    receive_cross(4)
-    select(1, sel_b, 8, 16)
     receive_cross(5)
+    project(1, 0, 4)
+    receive_cross(6)
+    select(1, sel_b, 0, 16)
     fill_signs(mix_a, rank_index(0), 7)
     fill_signs(mix_b, rank_index(1), 7)
-    receive_cross(6)
     loads[2].wait()
     prepare_scores()
     loads[3].wait()
@@ -470,6 +503,11 @@
     for copy in sent:
         copy.wait_send()
 
+    @pl.when(inner)
+    def _():
+        for copy in sent_inner:
+            copy.wait_send()
+
 
 def per_device(
     activations,
@@ -484,16 +522,21 @@
     val_feats,
 ):
     examples = lengths.shape[1]
-    smem = pl.BlockSpec(memory_space=pltpu.SMEM)
     vmem = pl.BlockSpec(memory_space=pltpu.VMEM)
     hbm = pl.BlockSpec(memory_space=pl.ANY)
     dma = pltpu.SemaphoreType.DMA
     return pl.pallas_call(
         kernel,
         out_shape=jax.ShapeDtypeStruct((1, examples, VALS), F32),
-        in_specs=[smem] * 2 + [vmem] * 4 + [hbm] * 4,
+        in_specs=[hbm] * 10,
         out_specs=vmem,
         scratch_shapes=[
+            pltpu.SMEM(lengths.shape, jnp.int32),
+            pltpu.SMEM(layout.shape, jnp.int32),
+            pltpu.VMEM(feature_signs.shape, jnp.int32),
+            pltpu.VMEM(rank_signs.shape, jnp.int32),
+            pltpu.VMEM(hadamard_rows.shape, jnp.int32),
+            pltpu.VMEM(entry_pick.shape, jnp.int32),
             pltpu.VMEM((TOK, D_MODEL), BF16),
             pltpu.VMEM((TOK, D_MODEL), BF16),
             pltpu.VMEM((VALS, SLICE), F32),
@@ -511,12 +554,12 @@
             pltpu.VMEM((MEMBERS, 1, SLICE), F32),
             pltpu.VMEM((8, VALS + RANK), F32),
             pltpu.VMEM((MEMBERS, 8, VALS + RANK), F32),
-            dma((5,)),
+            dma((11,)),
         ]
-        + [dma((4,))] * 4
+        + [dma((6,))] * 4
         + [dma((MEMBERS,))] * 10,
         compiler_params=pltpu.CompilerParams(
-            collective_id=0, has_side_effects=True, vmem_limit_bytes=48 * 1024 * 1024
+            collective_id=0, has_side_effects=True, vmem_limit_bytes=60 * 1024 * 1024
         ),
         cost_estimate=pl.CostEstimate(
             flops=10_000_000_000, bytes_accessed=8_000_000, transcendentals=0

time: 65.7 us -> 53.1 us (0.81)
  local copies, waits for them, and re-layouts: 10.5 us -> 1.26 us
  Pallas kernels: 54.7 us -> 51.7 us
    unnamed x21 -> x1, local copies, waits for them, and re-layouts: 10.5 us -> 1.26 us
    pallas_call x1, Pallas kernels: 54.7 us -> 51.7 us  [per_device(): pl.pallas_call(kernel, out_shape=jax.ShapeDtypeStruct((1, examples, VALS)...]
where the time goes in v2:
time: 53.1 us; the launch traced here: 53 us
  Pallas kernels  51.7 us (97%)
  local copies, waits for them, and re-layouts  1.26 us (2%)
    pallas_call x1, Pallas kernels, per_device(): pl.pallas_call(kernel, out_shape=jax.ShapeDtypeStruct((1, examples, VALS)...  51.7 us
    unnamed x1, local copies, waits for them, and re-layouts  1.26 us

profile of v2, /device:TPU:0, one launch (start us, length us, event | category | flops | bytes accessed | tf_op | source)
XLA Modules:
  0.0 53.0 jit_solution(14354963759977243550)
XLA Ops:
  0.0 51.7 %shard_map.100 = f32[1,2,256]{2,1,0:T(2,128)} custom-call(s32[2,2]{1,0:T(2,128)} %lengths_hbm.1, s32[2,8]{1,0:T(2,128)} %layout_hbm.1, s32[2,8192]{1,0:T(2,128)} %signs_hbm.1, s32[2,128]{1,0:T(2,128)} %rank_hbm.1, s32[2,8192]{1,0:T(2,128)} %rows_hbm.1, s32[2,4096]{1,0:T(2,128)} %pick_hbm.1, bf16[1,128,8192]{2,1,0:T(8,128)(2,1)} %act_hbm.1, ...), custom_call_target="tpu_custom_call" | custom-call | flops 10000000000 | bytes 8000000 | tf_op jit(solution)/shard_map/pallas_call | solution.py:528
  51.7 1.3 %copy.12 = f32[1,2,256]{2,1,0:T(2,128)} copy(f32[1,2,256]{2,1,0:T(2,128)} %shard_map.100) | data formatting | bytes 4096

commit v3 on v2

--- a/solution.py
+++ b/solution.py
@@ -385,35 +385,38 @@
         load.wait()
     loads[0].wait()
     fill_signs(t_ref, rows_ref[0:1, 0:CAND], 10)
+    fill_inputs(0, act_ref)
     receive(0)
-    fill_inputs(0, act_ref)
     receive(1)
+    fill_signs(mix_a, rank_index(0), 7)
+    fill_signs(mix_b, rank_index(1), 7)
     project(0, 0, 2)
     receive(2)
+    loads[2].wait()
+    prepare_scores()
     project(0, 2, 4)
+    select(0, sel_a, 0, 4)
     receive(3)
+    select(0, sel_a, 4, 8)
+    receive(4)
     receive_cross(0)
-    select(0, sel_a, 0, 5)
-    receive(4)
+    select(0, sel_a, 8, 12)
+    receive(5)
     receive_cross(1)
-    select(0, sel_a, 5, 10)
-    receive(5)
-    receive_cross(2)
-    select(0, sel_a, 10, 16)
-    receive(6)
-    receive_cross(3)
+    select(0, sel_a, 12, 16)
     loads[1].wait()
     fill_signs(t_ref, rows_ref[1:2, 0:CAND], 10)
+    receive(6)
+    receive_cross(2)
+    fill_inputs(1, cot_ref)
+    receive_cross(3)
+    project(1, 0, 2)
     receive_cross(4)
-    fill_inputs(1, cot_ref)
+    project(1, 2, 4)
     receive_cross(5)
-    project(1, 0, 4)
+    select(1, sel_b, 0, 8)
     receive_cross(6)
-    select(1, sel_b, 0, 16)
-    fill_signs(mix_a, rank_index(0), 7)
-    fill_signs(mix_b, rank_index(1), 7)
-    loads[2].wait()
-    prepare_scores()
+    select(1, sel_b, 8, 16)
     loads[3].wait()
     loads[4].wait()
 

time: 53.1 us -> 50.4 us (0.949)
  Pallas kernels: 51.7 us -> 48.9 us
    pallas_call x1, Pallas kernels: 51.7 us -> 48.9 us  [per_device(): pl.pallas_call(kernel, out_shape=jax.ShapeDtypeStruct((1, examples, VALS)...]
where the time goes in v3:
time: 50.4 us; the launch traced here: 50.2 us
  Pallas kernels  48.9 us (97%)
  local copies, waits for them, and re-layouts  1.26 us (2%)
    pallas_call x1, Pallas kernels, per_device(): pl.pallas_call(kernel, out_shape=jax.ShapeDtypeStruct((1, examples, VALS)...  48.9 us
    unnamed x1, local copies, waits for them, and re-layouts  1.26 us

profile of v3, /device:TPU:0, one launch (start us, length us, event | category | flops | bytes accessed | tf_op | source)
XLA Modules:
  0.0 50.2 jit_solution(9347272153338293269)
XLA Ops:
  0.0 48.9 %shard_map.100 = f32[1,2,256]{2,1,0:T(2,128)} custom-call(s32[2,2]{1,0:T(2,128)} %lengths_hbm.1, s32[2,8]{1,0:T(2,128)} %layout_hbm.1, s32[2,8192]{1,0:T(2,128)} %signs_hbm.1, s32[2,128]{1,0:T(2,128)} %rank_hbm.1, s32[2,8192]{1,0:T(2,128)} %rows_hbm.1, s32[2,4096]{1,0:T(2,128)} %pick_hbm.1, bf16[1,128,8192]{2,1,0:T(8,128)(2,1)} %act_hbm.1, ...), custom_call_target="tpu_custom_call" | custom-call | flops 10000000000 | bytes 8000000 | tf_op jit(solution)/shard_map/pallas_call | solution.py:531
  48.9 1.3 %copy.12 = f32[1,2,256]{2,1,0:T(2,128)} copy(f32[1,2,256]{2,1,0:T(2,128)} %shard_map.100) | data formatting | bytes 4096
